TPU v7x, 32 devices: a whole 2x2x4 slice. The times are simulated.
32 devices in a mesh: grp: 2 (over y), seq: 4 (over z), sub: 4 (over x, core).
Axes of the slice: x: 2, y: 2, z: 4, core: 2. Of those that a mesh axis runs over, the one named last changes fastest.
Arguments:
- queries: bfloat16 [1024, 4096], P(('grp', 'seq'), 'sub'), parts along dimension 0, may hold values from -6 to 6
- keys: bfloat16 [1024, 1024], P(('grp', 'seq'), 'sub'), parts along dimension 0, may hold values from -6 to 6
- values: bfloat16 [1024, 1024], P(('grp', 'seq'), 'sub'), parts along dimension 0, may hold values from -6 to 6
- output_gradient: bfloat16 [1024, 4096], P(('grp', 'seq'), 'sub'), parts along dimension 0, may hold values from -6 to 6
- doc_tiles: int32 [4], P('grp'), parts along dimension 0, may hold values from 1 to 24, 32 in all
Outputs:
- attended: bfloat16 [1024, 4096], P(('grp', 'seq'), 'sub'), parts along dimension 0
- query_grad: bfloat16 [1024, 4096], P(('grp', 'seq'), 'sub'), parts along dimension 0
- key_gradient: bfloat16 [1024, 1024], P(('grp', 'seq'), 'sub'), parts along dimension 0
- value_gradient: bfloat16 [1024, 1024], P(('grp', 'seq'), 'sub'), parts along dimension 0
There are 2 independent parts, one for each index of `grp`. A program takes and returns all parts, laid end to end along the dimension named above; each array names one. Nothing has to cross between parts.
Inputs may be any that keep to these rules, and one draw needn't show every extreme that they name: `doc_tiles`: the lengths sum to 32.
All inputs are finite; a program needn't handle non-finite values.
Results may differ from a plain program's by a relative error of at most 0.012.
The roundings to bfloat16 on the way count: a program that leaves them out, or rounds other values in their place, can miss the bound.
Values may be sent and summed in bfloat16 or wider, within the bound.
A program may use at most 64 MiB of HBM per device.

v0:
```python
import jax
import jax.numpy as jnp
from jax import lax
from jax.sharding import PartitionSpec as P

HEAD_SIZE = 128
TILE = 16
KB = 128


very_negative = -1e30


def tile_firsts(doc_tiles, total_tiles):
    doc_ends = jnp.cumsum(doc_tiles)
    begins = doc_ends - doc_tiles
    tile_ids = jnp.arange(total_tiles, dtype=jnp.int32)
    inside = begins[None, :] <= tile_ids[:, None]
    return jnp.max(jnp.where(inside, begins[None, :], 0), axis=1)


def balance(first_tiles, servers, per_source, capacity):
    total_tiles = first_tiles.shape[0]
    tile_ids = jnp.arange(total_tiles, dtype=jnp.int32)
    weights = tile_ids - first_tiles + 1
    tile_order = jnp.argsort(-weights, stable=True)

    def settle(carry_state, tile_id):
        server_load, pair_used = carry_state
        source = tile_id // per_source
        pair_row = lax.dynamic_index_in_dim(pair_used, source, 0, keepdims=False)
        choose_score = server_load + jnp.where(pair_row >= capacity, 1 << 30, 0)
        target = jnp.argmin(choose_score)
        server_load = server_load.at[target].add(weights[tile_id])
        pair_used = pair_used.at[source, target].add(1)
        return ((server_load, pair_used), target)

    start_state = (jnp.zeros((servers,), jnp.int32), jnp.zeros((servers, servers), jnp.int32))
    _, targets = lax.scan(settle, start_state, tile_order)
    return jnp.zeros((total_tiles,), jnp.int32).at[tile_order].set(targets)


def grouped(slot_rows, kv_heads):
    slot_count, tile_len, row_width = slot_rows.shape
    reshaped = slot_rows.reshape(
        slot_count, tile_len, kv_heads, row_width // (kv_heads * HEAD_SIZE), HEAD_SIZE
    )
    return reshaped.transpose(0, 2, 1, 3, 4).reshape(slot_count, kv_heads, -1, HEAD_SIZE)


def ungrouped(arranged, tile_len):
    slot_count, kv_heads, rows_all, head_dim = arranged.shape
    reshaped = arranged.reshape(slot_count, kv_heads, tile_len, rows_all // tile_len, head_dim)
    return reshaped.transpose(0, 2, 1, 3, 4).reshape(slot_count, tile_len, -1)


def block_span(first_key, stop_key, piece_start, piece_rows):
    first_block = jnp.maximum(first_key // KB, piece_start // KB)
    stop_block = jnp.minimum((stop_key - 1) // KB + 1, (piece_start + piece_rows) // KB)
    return (first_block, jnp.maximum(stop_block, first_block))


def block_scores(query_group, key_block, block_id, tile_id, first_key):
    kv_heads = query_group.shape[0]
    key_group = key_block.reshape(KB, kv_heads, HEAD_SIZE)
    scores = jnp.einsum(
        "gqd,kgd->gqk", query_group, key_group, preferred_element_type=jnp.float32
    ) * HEAD_SIZE ** (-0.5)
    row_count = query_group.shape[1]
    query_pos = tile_id * TILE + jnp.arange(row_count, dtype=jnp.int32) // (row_count // TILE)
    key_pos = block_id * KB + jnp.arange(KB, dtype=jnp.int32)
    allowed = (key_pos[None, :] >= first_key) & (key_pos[None, :] <= query_pos[:, None])
    return (scores, key_group, allowed)


def key_value_terms(
    query_group,
    grad_group,
    lse_rows,
    delta_slot,
    key_block,
    value_block,
    block_id,
    tile_id,
    first_key,
):
    kv_heads = query_group.shape[0]
    scores, key_group, allowed = block_scores(query_group, key_block, block_id, tile_id, first_key)
    value_group = value_block.reshape(KB, kv_heads, HEAD_SIZE)
    probs_exact = jnp.where(allowed, jnp.exp(scores - lse_rows[..., None]), 0.0)
    probs_bf = probs_exact.astype(jnp.bfloat16)
    prob_grad = jnp.einsum(
        "gqd,kgd->gqk", grad_group, value_group, preferred_element_type=jnp.float32
    )
    score_grad = (probs_exact * (prob_grad - delta_slot[..., None])).astype(jnp.bfloat16)
    return (score_grad, probs_bf, key_group)


def score_fold(query_groups, tile_ids, slot_count, first_tiles):

    def fold(carry_state, key_piece, piece_start):
        piece_rows = key_piece.shape[0]

        def per_slot(slot_id, inner_state):
            running_max, running_sum = inner_state
            tile_id = tile_ids[slot_id]
            first_key = first_tiles[tile_id] * TILE
            first_block, stop_block = block_span(
                first_key, (tile_id + 1) * TILE, piece_start, piece_rows
            )
            query_group = query_groups[slot_id]

            def per_block(block_id, row_state):
                row_max, row_sum = row_state
                key_block = lax.dynamic_slice_in_dim(key_piece, block_id * KB, KB, 0)
                scores, _, allowed = block_scores(
                    query_group, key_block, block_id, tile_id, first_key
                )
                masked = jnp.where(allowed, scores, very_negative)
                new_max = jnp.maximum(row_max, jnp.max(masked, axis=2))
                kept = jnp.where(allowed, jnp.exp(masked - new_max[..., None]), 0.0)
                return (new_max, row_sum * jnp.exp(row_max - new_max) + jnp.sum(kept, axis=2))

            row_state = lax.fori_loop(
                first_block, stop_block, per_block, (running_max[slot_id], running_sum[slot_id])
            )
            return (
                running_max.at[slot_id].set(row_state[0]),
                running_sum.at[slot_id].set(row_state[1]),
            )

        return lax.fori_loop(0, slot_count, per_slot, carry_state)

    return fold


def value_fold(query_groups, tile_ids, slot_count, first_tiles, row_lse):

    def fold(accum_state, kv_piece, piece_start):
        key_piece, value_piece = kv_piece
        piece_rows = key_piece.shape[0]
        kv_heads = query_groups.shape[1]

        def per_slot(slot_id, slot_accums):
            tile_id = tile_ids[slot_id]
            first_key = first_tiles[tile_id] * TILE
            first_block, stop_block = block_span(
                first_key, (tile_id + 1) * TILE, piece_start, piece_rows
            )
            query_group = query_groups[slot_id]
            lse_rows = row_lse[slot_id]

            def per_block(block_id, slot_accum):
                offset = block_id * KB
                key_block = lax.dynamic_slice_in_dim(key_piece, offset, KB, 0)
                value_block = lax.dynamic_slice_in_dim(value_piece, offset, KB, 0)
                scores, _, allowed = block_scores(
                    query_group, key_block, block_id, tile_id, first_key
                )
                probs_bf = jnp.where(allowed, jnp.exp(scores - lse_rows[..., None]), 0.0).astype(
                    jnp.bfloat16
                )
                value_group = value_block.reshape(KB, kv_heads, HEAD_SIZE)
                return slot_accum + jnp.einsum(
                    "gqk,kgd->gqd", probs_bf, value_group, preferred_element_type=jnp.float32
                )

            slot_accum = lax.fori_loop(first_block, stop_block, per_block, slot_accums[slot_id])
            return slot_accums.at[slot_id].set(slot_accum)

        return lax.fori_loop(0, slot_count, per_slot, accum_state)

    return fold


def grad_fold(query_groups, grad_groups, tile_ids, slot_count, first_tiles, row_lse, delta_rows):

    def fold(carry_state, kv_piece, piece_start):
        key_piece, value_piece = kv_piece
        piece_rows = key_piece.shape[0]

        def per_slot(slot_id, slot_state):
            query_accum, key_value_accum = slot_state
            tile_id = tile_ids[slot_id]
            first_key = first_tiles[tile_id] * TILE
            first_block, stop_block = block_span(
                first_key, (tile_id + 1) * TILE, piece_start, piece_rows
            )
            query_group = query_groups[slot_id]
            grad_group = grad_groups[slot_id]
            lse_rows = row_lse[slot_id]
            delta_slot = delta_rows[slot_id]

            def per_block(block_id, block_state):
                row_accum, kv_accum = block_state
                offset = block_id * KB
                key_block = lax.dynamic_slice_in_dim(key_piece, offset, KB, 0)
                value_block = lax.dynamic_slice_in_dim(value_piece, offset, KB, 0)
                score_grad, probs_bf, key_group = key_value_terms(
                    query_group,
                    grad_group,
                    lse_rows,
                    delta_slot,
                    key_block,
                    value_block,
                    block_id,
                    tile_id,
                    first_key,
                )
                row_accum = row_accum + jnp.einsum(
                    "gqk,kgd->gqd", score_grad, key_group, preferred_element_type=jnp.float32
                )
                key_part = jnp.einsum(
                    "gqk,gqd->kgd", score_grad, query_group, preferred_element_type=jnp.float32
                ).reshape(KB, -1)
                value_part = jnp.einsum(
                    "gqk,gqd->kgd", probs_bf, grad_group, preferred_element_type=jnp.float32
                ).reshape(KB, -1)
                current = lax.dynamic_slice_in_dim(kv_accum, block_id * KB, KB, 0)
                updated = current + jnp.concatenate([key_part, value_part], axis=1)
                kv_accum = lax.dynamic_update_slice_in_dim(kv_accum, updated, block_id * KB, 0)
                return (row_accum, kv_accum)

            row_accum, key_value_accum = lax.fori_loop(
                first_block, stop_block, per_block, (query_accum[slot_id], key_value_accum)
            )
            return (query_accum.at[slot_id].set(row_accum), key_value_accum)

        return lax.fori_loop(0, slot_count, per_slot, carry_state)

    return fold


def forward(query_slots, tile_ids, slot_count, first_tiles, keys, values):
    kv_heads = keys.shape[1] // HEAD_SIZE
    query_groups = grouped(query_slots, kv_heads)
    stat_shape = query_groups.shape[:3]
    stats_init = (
        jnp.full(stat_shape, very_negative, jnp.float32),
        jnp.zeros(stat_shape, jnp.float32),
    )
    score_step = score_fold(query_groups, tile_ids, slot_count, first_tiles)
    running_max, running_sum = score_step(
        stats_init, lax.all_gather(keys, "seq", axis=0, tiled=True), jnp.int32(0)
    )
    row_lse = running_max + jnp.log(running_sum)
    value_step = value_fold(query_groups, tile_ids, slot_count, first_tiles, row_lse)
    accum_init = jnp.zeros(query_groups.shape, jnp.float32)
    accum = value_step(
        accum_init,
        (
            lax.all_gather(keys, "seq", axis=0, tiled=True),
            lax.all_gather(values, "seq", axis=0, tiled=True),
        ),
        jnp.int32(0),
    )
    attended_slots = ungrouped(accum, query_slots.shape[1]).astype(jnp.bfloat16)
    return (query_groups, row_lse, attended_slots)


def row_deltas(attended_slots, grad_slots, kv_heads):
    grad_groups = grouped(grad_slots, kv_heads)
    attended_groups = grouped(attended_slots, kv_heads)
    return (
        grad_groups,
        jnp.sum(attended_groups.astype(jnp.float32) * grad_groups.astype(jnp.float32), axis=3),
    )


def backward(
    query_groups,
    grad_slots,
    attended_slots,
    tile_ids,
    slot_count,
    first_tiles,
    row_lse,
    keys,
    values,
    total_rows,
):
    kv_heads = query_groups.shape[1]
    grad_groups, delta_rows = row_deltas(attended_slots, grad_slots, kv_heads)
    grad_step = grad_fold(
        query_groups, grad_groups, tile_ids, slot_count, first_tiles, row_lse, delta_rows
    )
    grad_init = (
        jnp.zeros(query_groups.shape, jnp.float32),
        jnp.zeros((total_rows, 2 * kv_heads * HEAD_SIZE), jnp.float32),
    )
    query_accum, key_value_accum = grad_step(
        grad_init,
        (
            lax.all_gather(keys, "seq", axis=0, tiled=True),
            lax.all_gather(values, "seq", axis=0, tiled=True),
        ),
        jnp.int32(0),
    )
    query_slots_grad = ungrouped(query_accum * HEAD_SIZE ** (-0.5), grad_slots.shape[1]).astype(
        jnp.bfloat16
    )
    return (query_slots_grad, key_value_accum)


def per_device(queries, keys, values, output_gradient, doc_tiles):
    servers = lax.axis_size("seq")
    seq_index = lax.axis_index("seq")
    row_width = queries.shape[1]
    per_tile = queries.shape[0] // TILE
    total_tiles = per_tile * servers
    total_rows = queries.shape[0] * servers
    first_tiles = tile_firsts(doc_tiles, total_tiles)
    own_tiles = seq_index * per_tile + jnp.arange(per_tile, dtype=jnp.int32)
    query_tiles = queries.reshape(per_tile, TILE, row_width)
    grad_tiles = output_gradient.reshape(per_tile, TILE, row_width)
    capacity = max(1, 2 * per_tile // servers)
    slots_total = servers * capacity
    targets = balance(first_tiles, servers, per_tile, capacity)
    dest_server = lax.dynamic_slice_in_dim(targets, seq_index * per_tile, per_tile)
    tile_range = jnp.arange(per_tile, dtype=jnp.int32)
    earlier = tile_range[None, :] < tile_range[:, None]
    dest_rank = jnp.sum(earlier & (dest_server[None, :] == dest_server[:, None]), axis=1)
    slot_of = dest_server * capacity + dest_rank
    pick_table = jnp.arange(slots_total, dtype=jnp.int32)[:, None] == slot_of[None, :]
    pick_bf = pick_table.astype(jnp.bfloat16)

    def pack(tile_rows):
        flattened = tile_rows.reshape(per_tile, TILE * row_width)
        packed = jnp.dot(pick_bf, flattened, preferred_element_type=jnp.float32)
        return packed.astype(jnp.bfloat16).reshape(slots_total, TILE, row_width)

    def unpack(slot_rows):
        flattened = slot_rows.reshape(slots_total, TILE * row_width)
        unpacked = jnp.dot(pick_bf.T, flattened, preferred_element_type=jnp.float32)
        return unpacked.astype(jnp.bfloat16).reshape(per_tile * TILE, row_width)

    labels = jnp.sum(jnp.where(pick_table, own_tiles[None, :] + 1, 0), axis=1) - 1
    got_queries, got_labels = (
        lax.all_to_all(pack(query_tiles), "seq", split_axis=0, concat_axis=0, tiled=True),
        lax.all_to_all(labels, "seq", split_axis=0, concat_axis=0, tiled=True),
    )
    slot_range = jnp.arange(slots_total, dtype=jnp.int32)
    slot_order = jnp.argsort(
        jnp.where(got_labels >= 0, 0, 1) * slots_total + slot_range, stable=True
    )
    restore = jnp.argsort(slot_order)
    tile_ids = got_labels[slot_order]
    slot_count = jnp.sum((got_labels >= 0).astype(jnp.int32))
    query_groups, row_lse, attended_slots = forward(
        got_queries[slot_order], tile_ids, slot_count, first_tiles, keys, values
    )
    returned = lax.all_to_all(
        attended_slots[restore], "seq", split_axis=0, concat_axis=0, tiled=True
    )
    attended = unpack(returned)
    grad_slots = lax.all_to_all(pack(grad_tiles), "seq", split_axis=0, concat_axis=0, tiled=True)[
        slot_order
    ]
    query_slots_grad, key_value_accum = backward(
        query_groups,
        grad_slots,
        attended_slots,
        tile_ids,
        slot_count,
        first_tiles,
        row_lse,
        keys,
        values,
        total_rows,
    )
    grads_home = lax.all_to_all(
        query_slots_grad[restore], "seq", split_axis=0, concat_axis=0, tiled=True
    )
    query_grad = unpack(grads_home)
    half_width = keys.shape[1]
    summed = lax.psum_scatter(key_value_accum, "seq", scatter_dimension=0, tiled=True)
    key_gradient = (summed[:, :half_width] * HEAD_SIZE ** (-0.5)).astype(jnp.bfloat16)
    value_gradient = summed[:, half_width:].astype(jnp.bfloat16)
    return (attended, query_grad, key_gradient, value_gradient)


def solution(mesh):
    in_specs = (
        P(("grp", "seq"), "sub"),
        P(("grp", "seq"), "sub"),
        P(("grp", "seq"), "sub"),
        P(("grp", "seq"), "sub"),
        P("grp"),
    )
    out_specs = (
        P(("grp", "seq"), "sub"),
        P(("grp", "seq"), "sub"),
        P(("grp", "seq"), "sub"),
        P(("grp", "seq"), "sub"),
    )
    return jax.shard_map(
        per_device, mesh=mesh, in_specs=in_specs, out_specs=out_specs, check_vma=False
    )
```

profile of v0, /device:TPU:0, one launch (start us, length us, event | category | flops | bytes accessed | tf_op | source)
XLA Modules:
  0.0 725.8 jit_solution(15927289638018637415)
XLA Ops:
  8.1 1.6 sort.51
  9.8 362.3 %while.147 = (s32[]{:T(128)}, s32[4]{0:T(128)S(1)}, s32[4,4]{1,0:T(4,128)S(1)}, s32[32]{0:T(128)S(1)}, s32[32]{0:T(128)S(1)}, /*index=5*/s32[32]{0:T(128)S(1)}, s32[1,1]{1,0:T(1,128)}) while((s32[]{:T(128)}, s32[4]{0:T(128)S(1)}, s32[4,4]{1,0:T(4,128)S(1)}, s32[32]{0:T(128)S(1)}, s32[32]{0:T(128)S(1)}, /*index=5*/s32[32]{0:T(128)S(1)}, ...), condition=%wide.region_6.7_spmd.clone, body=%wide.region_3.6_spmd.sunk.clone | while | flops 74 | bytes 502 | solution.py:39
  373.8 6.3 all-to-all-start
  383.8 1.8 all-to-all-done
  385.6 3.5 all-to-all-start.1
  389.1 20.6 %all_gather.4 = bf16[512,256]{0,1:T(8,128)(2,1)S(1)} all-gather(bf16[128,256]{0,1:T(8,128)(2,1)S(1)} %copy.83), channel_id=1, replica_groups=mesh['grp'=2,'seq'=4,'sub'=4] {'seq'}, dimensions={0}, use_global_device_ids=true | all-gather | bytes 327680 | tf_op jit(solution)/shard_map/all_gather | solution.py:244
  410.9 13.0 %all_gather.10 = bf16[512,256]{0,1:T(8,128)(2,1)S(1)} all-gather(bf16[128,256]{0,1:T(8,128)(2,1)S(1)} %copy.84), channel_id=1, replica_groups=mesh['grp'=2,'seq'=4,'sub'=4] {'seq'}, dimensions={0}, use_global_device_ids=true | all-gather | bytes 327680 | tf_op jit(solution)/shard_map/all_gather | solution.py:253
  429.0 3.5 all-to-all-start.3
  434.5 63.9 %while.149 = (s32[]{:T(128)}, f32[16,2,64]{2,1,0:T(2,128)S(1)}, f32[16,2,64]{2,1,0:T(2,128)S(1)}, s32[]{:T(128)}, s32[16]{0:T(128)S(1)}, /*index=5*/s32[32]{0:T(...) while((s32[]{:T(128)}, f32[16,2,64]{2,1,0:T(2,128)S(1)}, ...), condition=%wide.region_18.19_spmd.clone, body=%wide.region_12.18_spmd.sunk.clone | while | flops 4310534 | bytes 468214 | solution.py:132
  478.1 1.8 while.148
  486.7 1.8 while.148
  495.3 1.8 while.148
  501.5 77.0 %while.151 = (s32[]{:T(128)}, f32[16,2,64,128]{3,0,2,1:T(8,128)S(1)}, s32[]{:T(128)}, s32[16]{0:T(128)S(1)}, s32[32]{0:T(128)S(1)}, /*index=5*/bf16[16,2,64,128]...) while((s32[]{:T(128)}, ...), condition=%wide.region_23.24_spmd.clone, body=%wide.region_19.23_spmd.sunk.clone | while | flops 8504336 | bytes 1233170 | solution.py:171
  554.3 1.4 while.150
  556.4 1.3 scatter.41
  564.4 1.4 while.150
  566.5 1.3 scatter.41
  574.4 1.4 while.150
  580.1 81.9 %while.153 = (s32[]{:T(128)}, f32[16,2,64,128]{3,2,1,0:T(8,128)S(1)}, f32[512,512]{0,1:T(8,128)S(1)}, s32[]{:T(128)}, s32[16]{0:T(128)S(1)}, /*index=5*/s32[32]{...) while((s32[]{:T(128)}, ...), condition=%wide.region_30.31_spmd.clone, body=%wide.region_26.30_spmd.sunk.clone | while | flops 21267468 | bytes 2545502 | solution.py:229
  624.1 2.3 while.152
  634.4 3.5 while.152
  645.8 3.5 while.152
  657.3 3.5 while.152
  662.1 1.3 copy.93
  664.1 1.4 gather_fusion.2
  665.5 7.7 %all-to-all-start.2 = ((bf16[16,16,1024]{2,1,0:T(8,128)(2,1)}), bf16[16,16,1024]{2,1,0:T(8,128)(2,1)S(1)}, u32[]{:S(2)}, u32[]{:S(2)}) async-start(bf16[16,16,1024]{2,1,0:T(8,128)(2,1)} %gather_fusion.2), calls=%async_computation.2 | async-start | bytes 1048576 | tf_op jit(solution)/shard_map/all_to_all | solution.py:352
  673.9 1.4 gather_fusion.4
  675.3 23.0 %all-to-all-done.2 = bf16[16,16,1024]{2,1,0:T(8,128)(2,1)S(1)} async-done(((bf16[16,16,1024]{2,1,0:T(8,128)(2,1)}), bf16[16,16,1024]{2,1,0:T(8,128)(2,1)S(1)}, u32[]{:S(2)}, u32[]{:S(2)}) %all-to-all-start.2) | async-done | bytes 524320 | tf_op jit(solution)/shard_map/all_to_all | solution.py:352
  698.3 5.9 all-to-all-start.4
  705.6 8.9 %all-to-all-done.4 = bf16[16,16,1024]{2,1,0:T(8,128)(2,1)S(1)} async-done(((bf16[16,16,1024]{2,1,0:T(8,128)(2,1)}), bf16[16,16,1024]{2,1,0:T(8,128)(2,1)S(1)}, u32[]{:S(2)}, u32[]{:S(2)}) %all-to-all-start.4) | async-done | bytes 524320 | tf_op jit(solution)/shard_map/all_to_all | solution.py:371
  715.8 1.5 slice.137
  717.4 1.5 fusion.32
  (908 shorter events, 257.5 us)
Async XLA Ops:
  7.2 0.7 copy-start.6
  9.7 371.3 %copy-start.1 = (bf16[128,1024]{1,0:T(8,128)(2,1)S(1)}, bf16[128,1024]{1,0:T(8,128)(2,1)}, u32[]{:S(2)}) copy-start(bf16[128,1024]{1,0:T(8,128)(2,1)} %param.31) | copy-start | bytes 786436
  373.8 11.8 %all-to-all-start = ((s32[4,4,1]{1,2,0:T(1,128)}), s32[4,4,1]{1,2,0:T(1,128)S(1)}, u32[]{:S(2)}, u32[]{:S(2)}) async-start(s32[4,4,1]{1,2,0:T(1,128)} %bitcast.45), calls=%async_computation | async-start | bytes 4096 | tf_op jit(solution)/shard_map/all_to_all | solution.py:340
  381.2 1.0 copy-start.2
  385.6 43.4 %all-to-all-start.1 = ((bf16[16,16,1024]{2,1,0:T(8,128)(2,1)}), bf16[16,16,1024]{2,1,0:T(8,128)(2,1)S(1)}, u32[]{:S(2)}, u32[]{:S(2)}) async-start(bf16[16,16,1024]{2,1,0:T(8,128)(2,1)} %bitcast.64), calls=%async_computation.1 | async-start | bytes 1048576 | tf_op jit(solution)/shard_map/all_to_all | solution.py:339
  389.1 20.7 %copy-start.3 = (bf16[128,256]{1,0:T(8,128)(2,1)S(1)}, bf16[128,256]{1,0:T(8,128)(2,1)}, u32[]{:S(2)}) copy-start(bf16[128,256]{1,0:T(8,128)(2,1)} %param.33) | copy-start | bytes 196612
  429.0 69.3 %all-to-all-start.3 = ((bf16[16,16,1024]{2,1,0:T(8,128)(2,1)}), bf16[16,16,1024]{2,1,0:T(8,128)(2,1)S(1)}, u32[]{:S(2)}, u32[]{:S(2)}) async-start(bf16[16,16,1024]{2,1,0:T(8,128)(2,1)} %bitcast.68), calls=%async_computation.3 | async-start | bytes 1048576 | tf_op jit(solution)/shard_map/all_to_all | solution.py:356
  432.5 283.3 %reduce-scatter.2.cloned.1.call-start = ((), (), s32[]{:S(2)}) async-start(), calls=%async_computation.6 | async-start | bytes 1310720 | tf_op jit(solution)/shard_map/reduce_scatter | solution.py:376
  433.8 0.7 copy-start.5
  500.9 0.7 copy-start.4
  578.5 0.8 copy-start
  665.5 32.8 %all-to-all-start.2 = ((bf16[16,16,1024]{2,1,0:T(8,128)(2,1)}), bf16[16,16,1024]{2,1,0:T(8,128)(2,1)S(1)}, u32[]{:S(2)}, u32[]{:S(2)}) async-start(bf16[16,16,1024]{2,1,0:T(8,128)(2,1)} %gather_fusion.2), calls=%async_computation.2 | async-start | bytes 1048576 | tf_op jit(solution)/shard_map/all_to_all | solution.py:352
  698.3 16.2 %all-to-all-start.4 = ((bf16[16,16,1024]{2,1,0:T(8,128)(2,1)}), bf16[16,16,1024]{2,1,0:T(8,128)(2,1)S(1)}, u32[]{:S(2)}, u32[]{:S(2)}) async-start(bf16[16,16,1024]{2,1,0:T(8,128)(2,1)} %gather_fusion.4), calls=%async_computation.4 | async-start | bytes 1048576 | tf_op jit(solution)/shard_map/all_to_all | solution.py:371
Sparse Core Ops, SparseCore 0:
  663.6 37.4 reduce-scatter.1
where the time goes:
time: 732 us; the launch traced here: 726 us
  loops' own time  359 us (49%)
  local copies, waits for them, and re-layouts  134 us (18%)
  other arithmetic  102 us (14%)
  waiting for transfers between devices  33.7 us (5%)
  blocking collectives  33.7 us (5%)
  starting transfers between devices  26.8 us (4%)
  matrix products  21.8 us (3%)
  between operations  14.4 us (2%)
    another operation x1, loops' own time, balance(): _, targets = lax.scan(settle, start_state, tile_order)  246 us
    another operation x2, loops' own time, fold(): return lax.fori_loop(0, slot_count, per_slot, carry_state)  72.3 us
    another operation x66, other arithmetic  49.2 us
    another operation x1, loops' own time, fold(): return lax.fori_loop(0, slot_count, per_slot, accum_state)  37.8 us
    dynamic_update_slice x32, local copies, waits for them, and re-layouts, balance(): _, targets = lax.scan(settle, start_state, tile_order)  24.3 us
    all_to_all x1, waiting for transfers between devices, per_device(): lax.all_to_all(attended_slots[restore], 'seq', split_axis=0, concat_axis=...  23 us
    another operation x32, other arithmetic, settle(): target = jnp.argmin(choose_score)  21.1 us
    all_gather x1, blocking collectives, forward(): lax.all_gather(keys, 'seq', axis=0, tiled=True)  20.6 us
  transfers between devices with their start and end apart: 6, of which 3 were waited for; matrix products, arithmetic and copies ran while one was open for 6% of the time, Pallas kernels for 0%

commit v1 on v0

v1 whole, which is shorter than its diff:
```python
import functools

import jax
import jax.numpy as jnp
from jax import lax
from jax.experimental import pallas as pl
from jax.experimental.pallas import tpu as pltpu
from jax.sharding import PartitionSpec as P

HEAD_SIZE = 128
TILE = 16
SCALE = HEAD_SIZE ** (-0.5)
VERY_NEGATIVE = -1e30
MESH = pl.DeviceIdType.MESH
F32 = jnp.float32
BF16 = jnp.bfloat16

NN = (((1,), (0,)), ((), ()))
NT = (((1,), (1,)), ((), ()))
TN = (((0,), (0,)), ((), ()))


def dot(a, b, dims):
    return lax.dot_general(a, b, dims, preferred_element_type=F32)


def kernel(
    n,
    doc_ref,
    q_ref,
    k_ref,
    v_ref,
    g_ref,
    att_ref,
    dq_ref,
    dk_ref,
    dv_ref,
    kv,
    qs,
    gs,
    gt,
    s_buf,
    dp_buf,
    m_buf,
    l_buf,
    o_buf,
    dq_buf,
    acc,
    outb,
    inb,
    up_send,
    up_recv,
    down_send,
    down_recv,
):
    me = lax.axis_index("seq")
    rows, width = q_ref.shape
    heads = k_ref.shape[1] // HEAD_SIZE
    rep = width // k_ref.shape[1]
    stacked = rep * rows
    last = n - 1
    above, below = lax.rem(me + 1, n), lax.rem(me + n - 1, n)

    def up(b, h):
        return pltpu.make_async_remote_copy(
            src_ref=kv.at[b, h],
            dst_ref=kv.at[b, h],
            send_sem=up_send.at[b, h],
            recv_sem=up_recv.at[b, h],
            device_id={"seq": above},
            device_id_type=MESH,
        )

    def down(b, h, kind):
        return pltpu.make_async_remote_copy(
            src_ref=outb.at[b, h, kind],
            dst_ref=inb.at[b, h, kind],
            send_sem=down_send.at[b, h, kind],
            recv_sem=down_recv.at[b, h, kind],
            device_id={"seq": below},
            device_id_type=MESH,
        )

    barrier = pltpu.get_barrier_semaphore()

    @pl.when(me < last)
    def _():
        pl.semaphore_signal(barrier, inc=1, device_id={"seq": above}, device_id_type=MESH)

    @pl.when(me > 0)
    def _():
        pl.semaphore_signal(barrier, inc=1, device_id={"seq": below}, device_id_type=MESH)

    for h in range(heads):
        kv[me, h, 0] = k_ref[:, h * HEAD_SIZE : (h + 1) * HEAD_SIZE]
        kv[me, h, 1] = v_ref[:, h * HEAD_SIZE : (h + 1) * HEAD_SIZE]

    inner = (me > 0) & (me < last)

    @pl.when(inner)
    def _():
        pl.semaphore_wait(barrier, 2)

    @pl.when(jnp.logical_not(inner))
    def _():
        pl.semaphore_wait(barrier, 1)

    @pl.when(me < last)
    def _():
        for h in range(heads):
            up(me, h).start()

    for h in range(heads):
        for r in range(rep):
            col = (h * rep + r) * HEAD_SIZE
            qs[h, r * rows : (r + 1) * rows] = q_ref[:, col : col + HEAD_SIZE]
            g_part = g_ref[:, col : col + HEAD_SIZE]
            gs[h, r * rows : (r + 1) * rows] = g_part
            gt[h, :, r * rows : (r + 1) * rows] = g_part.astype(F32).T

    column = lax.broadcasted_iota(jnp.int32, (1, stacked), 1)
    query_pos = me * rows + lax.rem(column, rows)
    first = jnp.zeros((1, stacked), jnp.int32)
    begin = jnp.int32(0)
    for d in range(doc_ref.shape[0]):
        first = jnp.where(begin <= query_pos, begin, first)
        begin = begin + doc_ref[d] * TILE
    key_row = lax.broadcasted_iota(jnp.int32, (rows, stacked), 0)

    for h in range(heads):
        m_buf[h] = jnp.full((1, stacked), VERY_NEGATIVE, F32)
        l_buf[h] = jnp.zeros((1, stacked), F32)
        o_buf[h] = jnp.zeros((HEAD_SIZE, stacked), F32)
        dq_buf[h] = jnp.zeros((HEAD_SIZE, stacked), F32)

    def arrive(t, carry):
        b = me - t

        @pl.when(t > 0)
        def _():
            for h in range(heads):
                up(b, h).wait_recv()

                @pl.when(me < last)
                def _():
                    up(b, h).start()

        key_pos = b * rows + key_row
        allowed = (key_pos >= first) & (key_pos <= query_pos)
        for h in range(heads):
            scores = dot(kv[b, h, 0], qs[h], NT) * SCALE
            scores = jnp.where(allowed, scores, VERY_NEGATIVE)
            s_buf[b, h] = scores
            old = m_buf[h]
            new = jnp.maximum(old, jnp.max(scores, axis=0, keepdims=True))
            total = jnp.sum(jnp.exp(scores - new), axis=0, keepdims=True)
            l_buf[h] = l_buf[h] * jnp.exp(old - new) + total
            m_buf[h] = new
            dp_buf[b, h] = dot(kv[b, h, 1], gs[h], NT)
        return carry

    lax.fori_loop(0, me + 1, arrive, 0)

    def emit(b, h, kind, part):
        goes = (me == last) & (b < me)

        @pl.when(goes)
        def _():
            outb[b, h, kind] = part.astype(outb.dtype)
            down(b, h, kind).start()

        @pl.when(jnp.logical_not(goes))
        def _():
            acc[b, h, kind] = part

    for h in range(heads):
        m_buf[h] = m_buf[h] + jnp.log(l_buf[h])

    def value_part(b, carry):
        for h in range(heads):
            probs = jnp.exp(s_buf[b, h] - m_buf[h])
            s_buf[b, h] = probs
            probs_bf = probs.astype(BF16)
            emit(b, h, 1, dot(probs_bf, gs[h], NN))
            o_buf[h] += dot(kv[b, h, 1], probs_bf, TN)
        return carry

    lax.fori_loop(0, me + 1, value_part, 0)

    for h in range(heads):
        rounded = o_buf[h].astype(BF16).astype(F32)
        l_buf[h] = jnp.sum(rounded * gt[h], axis=0, keepdims=True)

    def key_part(b, carry):
        for h in range(heads):
            score_grad = (s_buf[b, h] * (dp_buf[b, h] - l_buf[h])).astype(BF16)
            emit(b, h, 0, dot(score_grad, qs[h], NN))
            dq_buf[h] += dot(kv[b, h, 0], score_grad, TN)
        return carry

    lax.fori_loop(0, me + 1, key_part, 0)

    for h in range(heads):
        for r in range(rep):
            col = (h * rep + r) * HEAD_SIZE
            part = o_buf[h, :, r * rows : (r + 1) * rows]
            att_ref[:, col : col + HEAD_SIZE] = part.T.astype(BF16)
            part = dq_buf[h, :, r * rows : (r + 1) * rows] * SCALE
            dq_ref[:, col : col + HEAD_SIZE] = part.T.astype(BF16)

    def finish(h, kind, total):
        cols = slice(h * HEAD_SIZE, (h + 1) * HEAD_SIZE)
        if kind == 1:
            dv_ref[:, cols] = total.astype(BF16)
        else:
            dk_ref[:, cols] = (total * SCALE).astype(BF16)

    @pl.when(me < last)
    def _():
        for kind in (1, 0):

            def pass_on(b, carry):
                for h in range(heads):
                    down(b, h, kind).wait_recv()
                    outb[b, h, kind] = (
                        acc[b, h, kind] + inb[b, h, kind].astype(F32)
                    ).astype(outb.dtype)
                    down(b, h, kind).start()
                return carry

            lax.fori_loop(0, me, pass_on, 0)
            for h in range(heads):
                down(me, h, kind).wait_recv()
                finish(h, kind, acc[me, h, kind] + inb[me, h, kind].astype(F32))

    @pl.when(me == last)
    def _():
        for h in range(heads):
            for kind in (1, 0):
                finish(h, kind, acc[me, h, kind])

    @pl.when(me < last)
    def _():
        def sent(b, carry):
            for h in range(heads):
                up(b, h).wait_send()
            return carry

        lax.fori_loop(0, me + 1, sent, 0)

    def returned(b, carry):
        for h in range(heads):
            for kind in (1, 0):
                down(b, h, kind).wait_send()
        return carry

    lax.fori_loop(0, me, returned, 0)


def per_device(queries, keys, values, output_gradient, doc_tiles):
    n = lax.axis_size("seq")
    rows, width = queries.shape
    heads = keys.shape[1] // HEAD_SIZE
    stacked = rows * width // keys.shape[1]
    travel = BF16 if n <= 8 else F32
    vmem = pl.BlockSpec(memory_space=pltpu.VMEM)
    block = (n, heads, 2, rows, HEAD_SIZE)
    return pl.pallas_call(
        functools.partial(kernel, n),
        out_shape=(
            jax.ShapeDtypeStruct(queries.shape, BF16),
            jax.ShapeDtypeStruct(queries.shape, BF16),
            jax.ShapeDtypeStruct(keys.shape, BF16),
            jax.ShapeDtypeStruct(keys.shape, BF16),
        ),
        in_specs=[pl.BlockSpec(memory_space=pltpu.SMEM)] + [vmem] * 4,
        out_specs=(vmem,) * 4,
        scratch_shapes=[
            pltpu.VMEM(block, BF16),
            pltpu.VMEM((heads, stacked, HEAD_SIZE), BF16),
            pltpu.VMEM((heads, stacked, HEAD_SIZE), BF16),
            pltpu.VMEM((heads, HEAD_SIZE, stacked), F32),
            pltpu.VMEM((n, heads, rows, stacked), F32),
            pltpu.VMEM((n, heads, rows, stacked), F32),
            pltpu.VMEM((heads, 1, stacked), F32),
            pltpu.VMEM((heads, 1, stacked), F32),
            pltpu.VMEM((heads, HEAD_SIZE, stacked), F32),
            pltpu.VMEM((heads, HEAD_SIZE, stacked), F32),
            pltpu.VMEM(block, F32),
            pltpu.VMEM(block, travel),
            pltpu.VMEM(block, travel),
            pltpu.SemaphoreType.DMA((n, heads)),
            pltpu.SemaphoreType.DMA((n, heads)),
            pltpu.SemaphoreType.DMA((n, heads, 2)),
            pltpu.SemaphoreType.DMA((n, heads, 2)),
        ],
        compiler_params=pltpu.CompilerParams(
            collective_id=0, has_side_effects=True, vmem_limit_bytes=50 * 1024 * 1024
        ),
        cost_estimate=pl.CostEstimate(
            flops=12 * n * heads * rows * stacked * HEAD_SIZE,
            bytes_accessed=8 * rows * width,
            transcendentals=2 * n * heads * rows * stacked,
        ),
    )(doc_tiles, queries, keys, values, output_gradient)


def solution(mesh):
    rows = P(("grp", "seq"), "sub")
    return jax.shard_map(
        per_device,
        mesh=mesh,
        in_specs=(rows, rows, rows, rows, P("grp")),
        out_specs=(rows, rows, rows, rows),
        check_vma=False,
    )
```

time: 732 us -> 37 us (0.05)
  loops' own time: 359 us -> 0 us
  local copies, waits for them, and re-layouts: 134 us -> 6.89 us
  other arithmetic: 102 us -> 0 us
  blocking collectives: 33.7 us -> 0 us
  waiting for transfers between devices: 33.7 us -> 0 us
  Pallas kernels: 0 us -> 29.2 us
  starting transfers between devices: 26.8 us -> 0 us
  matrix products: 21.8 us -> 0 us
  between operations: 14.4 us -> 0.65 us
    another operation x28 -> x0, loops' own time: 359 us -> none  [the longest x1 246 us: balance(): _, targets = lax.scan(settle, start_state, tile_order)]
    another operation x98 -> x0, other arithmetic: 70.3 us -> none
    dynamic_slice x150 -> x0, local copies, waits for them, and re-layouts: 49 us -> none  [the longest x32 18.8 us: balance(): _, targets = lax.scan(settle, start_state, tile_order)]
    all_gather x2 -> x0, blocking collectives: 33.7 us -> none  [the longest x1 20.6 us: forward(): lax.all_gather(keys, 'seq', axis=0, tiled=True)]
    all_to_all x5 -> x0, waiting for transfers between devices: 33.7 us -> none  [the longest x1 23 us: per_device(): lax.all_to_all(attended_slots[restore], 'seq', split_axis=0, concat_axis=...]
    pallas_call x0 -> x1, Pallas kernels: none -> 29.2 us  [per_device(): pl.pallas_call(functools.partial(kernel, n), out_shape=(jax.ShapeDtypeStr...]
    all_to_all x5 -> x0, starting transfers between devices: 26.8 us -> none  [the longest x1 7.66 us: per_device(): lax.all_to_all(attended_slots[restore], 'seq', split_axis=0, concat_axis=...]
    dynamic_update_slice x32 -> x0, local copies, waits for them, and re-layouts: 24.3 us -> none  [balance(): _, targets = lax.scan(settle, start_state, tile_order)]
  transfers between devices with their start and end apart: 6 -> 0, of which waited for: 3 -> 0; matrix products, arithmetic and copies ran while one was open for 6% -> 0% of each run, Pallas kernels for 0% -> 0%
where the time goes in v1:
time: 37 us; the launch traced here: 36.7 us
  Pallas kernels  29.2 us (79%)
  local copies, waits for them, and re-layouts  6.89 us (19%)
  between operations  0.65 us (2%)
    pallas_call x1, Pallas kernels, per_device(): pl.pallas_call(functools.partial(kernel, n), out_shape=(jax.ShapeDtypeStr...  29.2 us
    unnamed x14, local copies, waits for them, and re-layouts  6.89 us

profile of v1, /device:TPU:0, one launch (start us, length us, event | category | flops | bytes accessed | tf_op | source)
XLA Modules:
  0.0 36.7 jit_solution(18147423545139411417)
XLA Ops:
  0.6 0.0 copy-start
  0.6 0.9 %copy-done = bf16[128,1024]{1,0:T(8,128)(2,1)S(1)} copy-done((bf16[128,1024]{1,0:T(8,128)(2,1)S(1)}, bf16[128,1024]{1,0:T(8,128)(2,1)}, u32[]{:S(2)}) %copy-start) | copy-done | bytes 262168
  1.6 0.0 copy-start.1
  1.6 0.9 %copy-done.1 = bf16[128,1024]{1,0:T(8,128)(2,1)S(1)} copy-done((bf16[128,1024]{1,0:T(8,128)(2,1)S(1)}, bf16[128,1024]{1,0:T(8,128)(2,1)}, u32[]{:S(2)}) %copy-start.1) | copy-done | bytes 262168
  2.5 0.0 copy-start.2
  2.5 0.8 %copy-done.2 = bf16[128,256]{1,0:T(8,128)(2,1)S(1)} copy-done((bf16[128,256]{1,0:T(8,128)(2,1)S(1)}, bf16[128,256]{1,0:T(8,128)(2,1)}, u32[]{:S(2)}) %copy-start.2) | copy-done | bytes 65560
  3.4 0.0 copy-start.3
  3.4 0.8 %copy-done.3 = bf16[128,256]{1,0:T(8,128)(2,1)S(1)} copy-done((bf16[128,256]{1,0:T(8,128)(2,1)S(1)}, bf16[128,256]{1,0:T(8,128)(2,1)}, u32[]{:S(2)}) %copy-start.3) | copy-done | bytes 65560
  4.2 0.0 copy-start.4
  4.2 0.7 %copy-done.4 = s32[2]{0:T(128)S(1)} copy-done((s32[2]{0:T(128)S(1)}, s32[2]{0:T(128)}, u32[]{:S(2)}) %copy-start.4) | copy-done | bytes 32
  4.9 29.2 %shard_map.84 = (bf16[128,1024]{1,0:T(8,128)(2,1)S(1)}, bf16[128,1024]{1,0:T(8,128)(2,1)S(1)}, bf16[128,256]{1,0:T(8,128)(2,1)S(1)}, bf16[128,256]{1,0:T(8,128)(2,1)S(1)}) custom-call(s32[2]{0:T(128)S(1)} %copy-done.4, bf16[128,1024]{1,0:T(8,128)(2,1)S(1)} %copy-done, bf16[128,256]{1,0:T(8,128)(2,1)S(1)} %copy-done.2, bf16[128,256]{1,0:T(8,128)(2,1)S(1)} %copy-done.3, ...), custom_call_target="tpu_custom_call" | custom-call | flops 805306368 | bytes 1048576 | tf_op jit(solution)/shard_map/pallas_call | solution.py:268
  34.1 0.7 %copy.13 = bf16[128,1024]{1,0:T(8,128)(2,1)} copy(bf16[128,1024]{1,0:T(8,128)(2,1)S(1)} %get-tuple-element.8) | data formatting | bytes 524288
  34.8 0.7 %copy.14 = bf16[128,1024]{1,0:T(8,128)(2,1)} copy(bf16[128,1024]{1,0:T(8,128)(2,1)S(1)} %get-tuple-element.9) | data formatting | bytes 524288
  35.5 0.6 %copy.15 = bf16[128,256]{1,0:T(8,128)(2,1)} copy(bf16[128,256]{1,0:T(8,128)(2,1)S(1)} %get-tuple-element.10) | data formatting | bytes 131072
  36.1 0.6 %copy.16 = bf16[128,256]{1,0:T(8,128)(2,1)} copy(bf16[128,256]{1,0:T(8,128)(2,1)S(1)} %get-tuple-element.11) | data formatting | bytes 131072
Async XLA Ops:
  0.6 1.0 %copy-start = (bf16[128,1024]{1,0:T(8,128)(2,1)S(1)}, bf16[128,1024]{1,0:T(8,128)(2,1)}, u32[]{:S(2)}) copy-start(bf16[128,1024]{1,0:T(8,128)(2,1)} %q_ref.1) | copy-start | bytes 786436
  1.6 0.9 %copy-start.1 = (bf16[128,1024]{1,0:T(8,128)(2,1)S(1)}, bf16[128,1024]{1,0:T(8,128)(2,1)}, u32[]{:S(2)}) copy-start(bf16[128,1024]{1,0:T(8,128)(2,1)} %g_ref.1) | copy-start | bytes 786436
  2.5 0.8 %copy-start.2 = (bf16[128,256]{1,0:T(8,128)(2,1)S(1)}, bf16[128,256]{1,0:T(8,128)(2,1)}, u32[]{:S(2)}) copy-start(bf16[128,256]{1,0:T(8,128)(2,1)} %k_ref.1) | copy-start | bytes 196612
  3.4 0.8 %copy-start.3 = (bf16[128,256]{1,0:T(8,128)(2,1)S(1)}, bf16[128,256]{1,0:T(8,128)(2,1)}, u32[]{:S(2)}) copy-start(bf16[128,256]{1,0:T(8,128)(2,1)} %v_ref.1) | copy-start | bytes 196612
  4.2 0.7 %copy-start.4 = (s32[2]{0:T(128)S(1)}, s32[2]{0:T(128)}, u32[]{:S(2)}) copy-start(s32[2]{0:T(128)} %doc_ref.1) | copy-start | bytes 28

commit v2 on v1

v2 whole, which is shorter than its diff:
```python
import functools

import jax
import jax.numpy as jnp
from jax import lax
from jax.experimental import pallas as pl
from jax.experimental.pallas import tpu as pltpu
from jax.sharding import PartitionSpec as P

HEAD_SIZE = 128
TILE = 16
SCALE = HEAD_SIZE ** (-0.5)
VERY_NEGATIVE = -1e30
VMEM_BYTES = 64 * 1024 * 1024
MESH = pl.DeviceIdType.MESH
F32 = jnp.float32
BF16 = jnp.bfloat16

NN = (((1,), (0,)), ((), ()))
NT = (((1,), (1,)), ((), ()))
TN = (((0,), (0,)), ((), ()))


def dot(a, b, dims):
    return lax.dot_general(a, b, dims, preferred_element_type=F32)


def loop(start, stop, body):
    if isinstance(start, int) and isinstance(stop, int):
        for x in range(start, stop):
            body(x)
    else:

        def step(x, carry):
            body(x)
            return carry

        lax.fori_loop(start, stop, step, 0)


def kernel(
    n,
    doc_hbm,
    q_ref,
    k_ref,
    v_ref,
    g_ref,
    att_hbm,
    dq_hbm,
    dk_hbm,
    dv_hbm,
    att_ref,
    dq_ref,
    dk_ref,
    dv_ref,
    doc_ref,
    kv,
    qs,
    gs,
    gt,
    s_buf,
    dp_buf,
    m_buf,
    l_buf,
    o_buf,
    dq_buf,
    acc,
    outb,
    inb,
    doc_sem,
    kv_sem,
    q_sem,
    up_send,
    up_recv,
    down_send,
    down_recv,
    out_sem,
):
    me = lax.axis_index("seq")
    rows, width = q_ref.shape
    heads = k_ref.shape[1] // HEAD_SIZE
    rep = width // k_ref.shape[1]
    stacked = rep * rows

    results = [
        pltpu.make_async_copy(src, dst, out_sem.at[i])
        for i, (src, dst) in enumerate(
            ((att_ref, att_hbm), (dq_ref, dq_hbm), (dk_ref, dk_hbm), (dv_ref, dv_hbm))
        )
    ]

    def head_cols(h):
        return slice(h * HEAD_SIZE, (h + 1) * HEAD_SIZE)

    def own_kv(h, kind):
        src = (k_ref, v_ref)[kind].at[:, head_cols(h)]
        return pltpu.make_async_copy(src, kv.at[me, h, kind], kv_sem.at[h, kind])

    def own_rows(h, r, kind):
        src = (q_ref, g_ref)[kind].at[:, head_cols(h * rep + r)]
        dst = (qs, gs)[kind].at[h, pl.ds(r * rows, rows)]
        return pltpu.make_async_copy(src, dst, q_sem.at[h, r, kind])

    barrier = pltpu.get_barrier_semaphore()
    for d in range(1, n):
        other = lax.rem(me + d, n)
        pl.semaphore_signal(barrier, inc=1, device_id={"seq": other}, device_id_type=MESH)

    pairs = [(h, kind) for h in range(heads) for kind in range(2)]
    for h, kind in pairs:
        own_kv(h, kind).start()
    doc_copy = pltpu.make_async_copy(doc_hbm, doc_ref, doc_sem)
    doc_copy.start()
    for h, kind in pairs:
        for r in range(rep):
            own_rows(h, r, kind).start()

    for h, kind in pairs:
        own_kv(h, kind).wait()
    pl.semaphore_wait(barrier, n - 1)

    def run(me):
        def up(src, target, h):
            return pltpu.make_async_remote_copy(
                src_ref=kv.at[src, h],
                dst_ref=kv.at[src, h],
                send_sem=up_send.at[target, h],
                recv_sem=up_recv.at[src, h],
                device_id={"seq": target},
                device_id_type=MESH,
            )

        def down(src, target, h, kind):
            return pltpu.make_async_remote_copy(
                src_ref=outb.at[target, h, kind],
                dst_ref=inb.at[src, h, kind],
                send_sem=down_send.at[target, h, kind],
                recv_sem=down_recv.at[src, h, kind],
                device_id={"seq": target},
                device_id_type=MESH,
            )

        for h in range(heads):
            loop(0, n - 1 - me, lambda x: up(me, n - 1 - x, h).start())

        doc_copy.wait()
        column = lax.broadcasted_iota(jnp.int32, (1, stacked), 1)
        query_pos = me * rows + lax.rem(column, rows)
        first = jnp.zeros((1, stacked), jnp.int32)
        begin = jnp.int32(0)
        for d in range(doc_ref.shape[0]):
            first = jnp.where(begin <= query_pos, begin, first)
            begin = begin + doc_ref[d] * TILE
        key_row = lax.broadcasted_iota(jnp.int32, (rows, stacked), 0)

        def scores_of(b, h):
            key_pos = b * rows + key_row
            allowed = (key_pos >= first) & (key_pos <= query_pos)
            scores = dot(kv[b, h, 0], qs[h], NT) * SCALE
            scores = jnp.where(allowed, scores, VERY_NEGATIVE)
            s_buf[b, h] = scores
            dp_buf[b, h] = dot(kv[b, h, 1], gs[h], NT)
            return scores, jnp.max(scores, axis=0, keepdims=True)

        for h in range(heads):
            for r in range(rep):
                for kind in range(2):
                    own_rows(h, r, kind).wait()
            scores, top = scores_of(me, h)
            m_buf[h] = top
            l_buf[h] = jnp.sum(jnp.exp(scores - top), axis=0, keepdims=True)
            gt[h] = gs[h].astype(F32).T
            o_buf[h] = jnp.zeros((HEAD_SIZE, stacked), F32)
            dq_buf[h] = jnp.zeros((HEAD_SIZE, stacked), F32)

        def emit(b, h, kind, part):
            outb[b, h, kind] = part.astype(BF16)
            down(me, b, h, kind).start()

        for h in range(heads):

            def arrive(t):
                b = me - t
                up(b, me, h).wait_recv()
                scores, top = scores_of(b, h)
                old = m_buf[h]
                new = jnp.maximum(old, top)
                total = jnp.sum(jnp.exp(scores - new), axis=0, keepdims=True)
                l_buf[h] = l_buf[h] * jnp.exp(old - new) + total
                m_buf[h] = new

            loop(1, me + 1, arrive)
            lse = m_buf[h] + jnp.log(l_buf[h])
            m_buf[h] = lse

            def value_part(b):
                probs = jnp.exp(s_buf[b, h] - m_buf[h])
                s_buf[b, h] = probs
                probs_bf = probs.astype(BF16)
                o_buf[h] += dot(kv[b, h, 1], probs_bf, TN)
                return dot(probs_bf, gs[h], NN)

            loop(0, me, lambda b: emit(b, h, 1, value_part(b)))
            acc[h, 1] = value_part(me)

            rounded = o_buf[h].astype(BF16).astype(F32)
            l_buf[h] = jnp.sum(rounded * gt[h], axis=0, keepdims=True)

            def key_part(b):
                score_grad = (s_buf[b, h] * (dp_buf[b, h] - l_buf[h])).astype(BF16)
                dq_buf[h] += dot(kv[b, h, 0], score_grad, TN)
                return dot(score_grad, qs[h], NN)

            loop(0, me, lambda b: emit(b, h, 0, key_part(b)))
            acc[h, 0] = key_part(me)

        for h in range(heads):
            for r in range(rep):
                part = o_buf[h, :, r * rows : (r + 1) * rows]
                att_ref[:, head_cols(h * rep + r)] = part.T.astype(BF16)
                part = dq_buf[h, :, r * rows : (r + 1) * rows] * SCALE
                dq_ref[:, head_cols(h * rep + r)] = part.T.astype(BF16)
        results[0].start()
        results[1].start()

        for h in range(heads):
            for kind in (1, 0):

                def add(x):
                    src = n - 1 - x
                    down(src, me, h, kind).wait_recv()
                    acc[h, kind] += inb[src, h, kind].astype(F32)

                loop(0, n - 1 - me, add)
                if kind == 1:
                    dv_ref[:, head_cols(h)] = acc[h, 1].astype(BF16)
                else:
                    dk_ref[:, head_cols(h)] = (acc[h, 0] * SCALE).astype(BF16)

        results[2].start()
        results[3].start()

        for h in range(heads):
            loop(0, n - 1 - me, lambda x: up(me, n - 1 - x, h).wait_send())
            for kind in (1, 0):
                loop(0, me, lambda b: down(me, b, h, kind).wait_send())
        for copy in results:
            copy.wait()

    if n <= 4:
        for i in range(n):
            pl.when(me == i)(functools.partial(run, i))
    else:
        run(me)


def write_out(*refs):
    count = len(refs) // 2
    sems = refs[-1]
    copies = [
        pltpu.make_async_copy(refs[i], refs[count + i], sems.at[i]) for i in range(count)
    ]
    for copy in copies:
        copy.start()
    for copy in copies:
        copy.wait()


def per_device(queries, keys, values, output_gradient, doc_tiles):
    n = lax.axis_size("seq")
    rows, width = queries.shape
    heads = keys.shape[1] // HEAD_SIZE
    rep = width // keys.shape[1]
    stacked = rows * rep
    hbm = pl.BlockSpec(memory_space=pltpu.HBM)
    block = (n, heads, 2, rows, HEAD_SIZE)
    shapes = (
        jax.ShapeDtypeStruct(queries.shape, BF16),
        jax.ShapeDtypeStruct(queries.shape, BF16),
        jax.ShapeDtypeStruct(keys.shape, BF16),
        jax.ShapeDtypeStruct(keys.shape, BF16),
    )
    dma = pltpu.SemaphoreType.DMA
    results = pl.pallas_call(
        functools.partial(kernel, n),
        out_shape=shapes,
        in_specs=[hbm] * 5,
        out_specs=(hbm,) * 4,
        scratch_shapes=[
            pltpu.VMEM(queries.shape, BF16),
            pltpu.VMEM(queries.shape, BF16),
            pltpu.VMEM(keys.shape, BF16),
            pltpu.VMEM(keys.shape, BF16),
            pltpu.SMEM(doc_tiles.shape, jnp.int32),
            pltpu.VMEM(block, BF16),
            pltpu.VMEM((heads, stacked, HEAD_SIZE), BF16),
            pltpu.VMEM((heads, stacked, HEAD_SIZE), BF16),
            pltpu.VMEM((heads, HEAD_SIZE, stacked), F32),
            pltpu.VMEM((n, heads, rows, stacked), F32),
            pltpu.VMEM((n, heads, rows, stacked), F32),
            pltpu.VMEM((heads, 1, stacked), F32),
            pltpu.VMEM((heads, 1, stacked), F32),
            pltpu.VMEM((heads, HEAD_SIZE, stacked), F32),
            pltpu.VMEM((heads, HEAD_SIZE, stacked), F32),
            pltpu.VMEM((heads, 2, rows, HEAD_SIZE), F32),
            pltpu.VMEM(block, BF16),
            pltpu.VMEM(block, BF16),
            dma,
            dma((heads, 2)),
            dma((heads, rep, 2)),
            dma((n, heads)),
            dma((n, heads)),
            dma((n, heads, 2)),
            dma((n, heads, 2)),
            dma((4,)),
        ],
        compiler_params=pltpu.CompilerParams(
            collective_id=0, has_side_effects=True, vmem_limit_bytes=VMEM_BYTES
        ),
        cost_estimate=pl.CostEstimate(
            flops=12 * n * heads * rows * stacked * HEAD_SIZE,
            bytes_accessed=8 * rows * width,
            transcendentals=2 * n * heads * rows * stacked,
        ),
    )(doc_tiles, queries, keys, values, output_gradient)
    return pl.pallas_call(
        write_out,
        out_shape=shapes,
        in_specs=[hbm] * 4,
        out_specs=(hbm,) * 4,
        scratch_shapes=[dma((4,))],
        compiler_params=pltpu.CompilerParams(vmem_limit_bytes=VMEM_BYTES),
    )(*results)


def solution(mesh):
    rows = P(("grp", "seq"), "sub")
    return jax.shard_map(
        per_device,
        mesh=mesh,
        in_specs=(rows, rows, rows, rows, P("grp")),
        out_specs=(rows, rows, rows, rows),
        check_vma=False,
    )
```

time: 37 us -> 49.4 us (1.34)
  Pallas kernels: 29.2 us -> 48.5 us
  local copies, waits for them, and re-layouts: 6.89 us -> 0 us
    pallas_call x1 -> x2, Pallas kernels: 29.2 us -> 48.5 us  [the longest x1 27.5 us: per_device(): pl.pallas_call(functools.partial(kernel, n), out_shape=shapes, in_specs=[...]
    unnamed x14 -> x0, local copies, waits for them, and re-layouts: 6.89 us -> none
where the time goes in v2:
time: 49.4 us; the launch traced here: 49.2 us
  Pallas kernels  48.5 us (98%)
  between operations  0.64 us (1%)
    pallas_call x1, Pallas kernels, per_device(): pl.pallas_call(functools.partial(kernel, n), out_shape=shapes, in_specs=[...  27.5 us
    pallas_call x1, Pallas kernels, per_device(): pl.pallas_call(write_out, out_shape=shapes, in_specs=[hbm] * 4, out_specs...  21 us

profile of v2, /device:TPU:0, one launch (start us, length us, event | category | flops | bytes accessed | tf_op | source)
XLA Modules:
  0.0 49.2 jit_solution(16845226012450807596)
XLA Ops:
  0.6 27.5 %shard_map.84 = (bf16[128,1024]{1,0:T(8,128)(2,1)}, bf16[128,1024]{1,0:T(8,128)(2,1)}, bf16[128,256]{1,0:T(8,128)(2,1)}, bf16[128,256]{1,0:T(8,128)(2,1)}) custom-call(s32[2]{0:T(128)} %doc_hbm.1, bf16[128,1024]{1,0:T(8,128)(2,1)} %q_ref.1, bf16[128,256]{1,0:T(8,128)(2,1)} %k_ref.1, bf16[128,256]{1,0:T(8,128)(2,1)} %v_ref.1, bf16[128,1024]{1,0:T(8,128)(2,1)} %g_ref.1), custom_call_target="tpu_custom_call" | custom-call | flops 805306368 | bytes 1048576 | tf_op jit(solution)/shard_map/pallas_call | solution.py:284
  28.2 21.0 %shard_map.85 = (bf16[128,1024]{1,0:T(8,128)(2,1)}, bf16[128,1024]{1,0:T(8,128)(2,1)}, bf16[128,256]{1,0:T(8,128)(2,1)}, bf16[128,256]{1,0:T(8,128)(2,1)}) custom-call(bf16[128,1024]{1,0:T(8,128)(2,1)} %get-tuple-element.8.refs_0_, bf16[128,1024]{1,0:T(8,128)(2,1)} %get-tuple-element.9.refs_1_, bf16[128,256]{1,0:T(8,128)(2,1)} %get-tuple-element.10.refs_2_, ...), custom_call_target="tpu_custom_call" | custom-call | tf_op jit(solution)/shard_map/pallas_call | solution.py:326

commit v3 on v2

--- a/solution.py
+++ b/solution.py
@@ -255,14 +255,19 @@
 
 
 def write_out(*refs):
-    count = len(refs) // 2
-    sems = refs[-1]
-    copies = [
-        pltpu.make_async_copy(refs[i], refs[count + i], sems.at[i]) for i in range(count)
+    count = 4
+    sources, targets, held = refs[:count], refs[count : 2 * count], refs[2 * count : 3 * count]
+    sems = refs[3 * count]
+    arriving = [
+        pltpu.make_async_copy(sources[i], held[i], sems.at[0, i]) for i in range(count)
     ]
-    for copy in copies:
+    leaving = [pltpu.make_async_copy(held[i], targets[i], sems.at[1, i]) for i in range(count)]
+    for copy in arriving:
         copy.start()
-    for copy in copies:
+    for i in range(count):
+        arriving[i].wait()
+        leaving[i].start()
+    for copy in leaving:
         copy.wait()
 
 
@@ -328,7 +333,7 @@
         out_shape=shapes,
         in_specs=[hbm] * 4,
         out_specs=(hbm,) * 4,
-        scratch_shapes=[dma((4,))],
+        scratch_shapes=[pltpu.VMEM(shape.shape, BF16) for shape in shapes] + [dma((2, 4))],
         compiler_params=pltpu.CompilerParams(vmem_limit_bytes=VMEM_BYTES),
     )(*results)
 

time: 49.4 us -> 30.2 us (0.61)
  Pallas kernels: 48.5 us -> 29.4 us
    pallas_call x1, Pallas kernels: 21 us -> 1.84 us  [per_device(): pl.pallas_call(write_out, out_shape=shapes, in_specs=[hbm] * 4, out_specs...]
where the time goes in v3:
time: 30.2 us; the launch traced here: 30 us
  Pallas kernels  29.4 us (97%)
  between operations  0.64 us (2%)
    pallas_call x1, Pallas kernels, per_device(): pl.pallas_call(functools.partial(kernel, n), out_shape=shapes, in_specs=[...  27.5 us
    pallas_call x1, Pallas kernels, per_device(): pl.pallas_call(write_out, out_shape=shapes, in_specs=[hbm] * 4, out_specs...  1.84 us

profile of v3, /device:TPU:0, one launch (start us, length us, event | category | flops | bytes accessed | tf_op | source)
XLA Modules:
  0.0 30.0 jit_solution(9370746161381335695)
XLA Ops:
  0.6 27.5 %shard_map.84 = (bf16[128,1024]{1,0:T(8,128)(2,1)}, bf16[128,1024]{1,0:T(8,128)(2,1)}, bf16[128,256]{1,0:T(8,128)(2,1)}, bf16[128,256]{1,0:T(8,128)(2,1)}) custom-call(s32[2]{0:T(128)} %doc_hbm.1, bf16[128,1024]{1,0:T(8,128)(2,1)} %q_ref.1, bf16[128,256]{1,0:T(8,128)(2,1)} %k_ref.1, bf16[128,256]{1,0:T(8,128)(2,1)} %v_ref.1, bf16[128,1024]{1,0:T(8,128)(2,1)} %g_ref.1), custom_call_target="tpu_custom_call" | custom-call | flops 805306368 | bytes 1048576 | tf_op jit(solution)/shard_map/pallas_call | solution.py:289
  28.2 1.8 %shard_map.85 = (bf16[128,1024]{1,0:T(8,128)(2,1)}, bf16[128,1024]{1,0:T(8,128)(2,1)}, bf16[128,256]{1,0:T(8,128)(2,1)}, bf16[128,256]{1,0:T(8,128)(2,1)}) custom-call(bf16[128,1024]{1,0:T(8,128)(2,1)} %get-tuple-element.8.refs_0_, bf16[128,1024]{1,0:T(8,128)(2,1)} %get-tuple-element.9.refs_1_, bf16[128,256]{1,0:T(8,128)(2,1)} %get-tuple-element.10.refs_2_, ...), custom_call_target="tpu_custom_call" | custom-call | tf_op jit(solution)/shard_map/pallas_call | solution.py:331

commit v4 on v3

--- a/solution.py
+++ b/solution.py
@@ -140,8 +140,26 @@
                 device_id_type=MESH,
             )
 
-        for h in range(heads):
-            loop(0, n - 1 - me, lambda x: up(me, n - 1 - x, h).start())
+        relayed = n == 4
+        skip = 1 if relayed and me == 0 else 0
+
+        def forward(h):
+            return pltpu.make_async_remote_copy(
+                src_ref=kv.at[0, h],
+                dst_ref=kv.at[0, h],
+                send_sem=up_send.at[0, h],
+                recv_sem=up_recv.at[0, h],
+                device_id={"seq": 3},
+                device_id_type=MESH,
+            )
+
+        def relay(h):
+            if relayed and me == 2:
+                up(0, me, h).wait_recv()
+                forward(h).start()
+
+        for h in range(heads):
+            loop(skip, n - 1 - me, lambda x: up(me, n - 1 - x, h).start())
 
         doc_copy.wait()
         column = lax.broadcasted_iota(jnp.int32, (1, stacked), 1)
@@ -177,11 +195,13 @@
             outb[b, h, kind] = part.astype(BF16)
             down(me, b, h, kind).start()
 
+        relay(0)
         for h in range(heads):
 
             def arrive(t):
                 b = me - t
-                up(b, me, h).wait_recv()
+                if not (relayed and me == 2 and b == 0):
+                    up(b, me, h).wait_recv()
                 scores, top = scores_of(b, h)
                 old = m_buf[h]
                 new = jnp.maximum(old, top)
@@ -202,6 +222,8 @@
 
             loop(0, me, lambda b: emit(b, h, 1, value_part(b)))
             acc[h, 1] = value_part(me)
+            if h + 1 < heads:
+                relay(h + 1)
 
             rounded = o_buf[h].astype(BF16).astype(F32)
             l_buf[h] = jnp.sum(rounded * gt[h], axis=0, keepdims=True)
@@ -241,7 +263,9 @@
         results[3].start()
 
         for h in range(heads):
-            loop(0, n - 1 - me, lambda x: up(me, n - 1 - x, h).wait_send())
+            loop(skip, n - 1 - me, lambda x: up(me, n - 1 - x, h).wait_send())
+            if relayed and me == 2:
+                forward(h).wait_send()
             for kind in (1, 0):
                 loop(0, me, lambda b: down(me, b, h, kind).wait_send())
         for copy in results:

time: 30.2 us -> 28.4 us (0.940)
  Pallas kernels: 29.4 us -> 27.5 us
    pallas_call x1, Pallas kernels: 27.5 us -> 25.7 us  [per_device(): pl.pallas_call(functools.partial(kernel, n), out_shape=shapes, in_specs=[...]
where the time goes in v4:
time: 28.4 us; the launch traced here: 28.1 us
  Pallas kernels  27.5 us (97%)
  between operations  0.64 us (2%)
    pallas_call x1, Pallas kernels, per_device(): pl.pallas_call(functools.partial(kernel, n), out_shape=shapes, in_specs=[...  25.7 us
    pallas_call x1, Pallas kernels, per_device(): pl.pallas_call(write_out, out_shape=shapes, in_specs=[hbm] * 4, out_specs...  1.84 us

profile of v4, /device:TPU:0, one launch (start us, length us, event | category | flops | bytes accessed | tf_op | source)
XLA Modules:
  0.0 28.1 jit_solution(2136062900637244338)
XLA Ops:
  0.6 25.7 %shard_map.84 = (bf16[128,1024]{1,0:T(8,128)(2,1)}, bf16[128,1024]{1,0:T(8,128)(2,1)}, bf16[128,256]{1,0:T(8,128)(2,1)}, bf16[128,256]{1,0:T(8,128)(2,1)}) custom-call(s32[2]{0:T(128)} %doc_hbm.1, bf16[128,1024]{1,0:T(8,128)(2,1)} %q_ref.1, bf16[128,256]{1,0:T(8,128)(2,1)} %k_ref.1, bf16[128,256]{1,0:T(8,128)(2,1)} %v_ref.1, bf16[128,1024]{1,0:T(8,128)(2,1)} %g_ref.1), custom_call_target="tpu_custom_call" | custom-call | flops 805306368 | bytes 1048576 | tf_op jit(solution)/shard_map/pallas_call | solution.py:313
  26.3 1.8 %shard_map.85 = (bf16[128,1024]{1,0:T(8,128)(2,1)}, bf16[128,1024]{1,0:T(8,128)(2,1)}, bf16[128,256]{1,0:T(8,128)(2,1)}, bf16[128,256]{1,0:T(8,128)(2,1)}) custom-call(bf16[128,1024]{1,0:T(8,128)(2,1)} %get-tuple-element.8.refs_0_, bf16[128,1024]{1,0:T(8,128)(2,1)} %get-tuple-element.9.refs_1_, bf16[128,256]{1,0:T(8,128)(2,1)} %get-tuple-element.10.refs_2_, ...), custom_call_target="tpu_custom_call" | custom-call | tf_op jit(solution)/shard_map/pallas_call | solution.py:355
